TPU v7x, 32 devices: a whole 2x2x4 slice. The times are simulated.
32 devices in a mesh: req: 2 (over y), ctx: 8 (over z, x), tp: 2 (over core).
Axes of the slice: x: 2, y: 2, z: 4, core: 2. Of those that a mesh axis runs over, the one named last changes fastest.
Arguments:
- hidden: bfloat16 [2048, 8192], P(('req', 'ctx')), parts along dimension 0, may hold values from -6 to 6
- suffix_hidden: bfloat16 [32, 8192], P(('req', 'ctx')), parts along dimension 0, may hold values from -6 to 6
- norm_gain: float32 [8192], replicated, may hold values from 0.1 to 1.9
- key_matrix: bfloat16 [8192, 512], P('ctx', 'tp'), may hold values from -0.0625 to 0.0625
- value_matrix: bfloat16 [8192, 512], P('ctx', 'tp'), may hold values from -0.0625 to 0.0625
- key_offset_bias: float32 [512], P('tp'), may hold values from -4 to 4
- value_offset_bias: float32 [512], P('tp'), may hold values from -4 to 4
- suffix_query_rows: bfloat16 [32, 4096], P(('req', 'ctx'), 'tp'), parts along dimension 0, may hold values from -100 to 100
- slot_keys: bfloat16 [64, 128, 512], P(('req', 'ctx'), None, 'tp'), parts along dimension 0, may hold values from -4 to 4
- slot_values: bfloat16 [64, 128, 512], P(('req', 'ctx'), None, 'tp'), parts along dimension 0, may hold values from -4 to 4
- page_slot_table: int32 [32], P('req'), parts along dimension 0, may hold values from 0 to 31, as said below
- split_page: int32 [2], P('req'), parts along dimension 0, may hold values from 4 to 8
Outputs:
- front_keys: bfloat16 [2048, 512], P(('req', 'ctx'), 'tp'), parts along dimension 0
- front_values: bfloat16 [2048, 512], P(('req', 'ctx'), 'tp'), parts along dimension 0
- attended: bfloat16 [32, 4096], P(('req', 'ctx'), 'tp'), parts along dimension 0
There are 2 independent parts, one for each index of `req`. A program takes and returns all parts, laid end to end along the dimension named above; an argument that names none is the same for every part. Nothing has to cross between parts.
Inputs may be any that keep to these rules, and one draw needn't show every extreme that they name: `page_slot_table`: distinct storage slots; slot s lies on ctx device s // 4; no device holds more than 4 pages of a group, and some device holds exactly 4.
All inputs are finite; a program needn't handle non-finite values.
Results may differ from a plain program's by a relative error of at most 0.0063.
Values may be sent and summed in bfloat16 or wider, within the bound.
No kernel may reach another device: no remote copies, remote signals or barrier semaphores. Data moves between devices by JAX's collectives and lax.ppermute only.
A program may use at most 64 MiB of HBM per device.

v0:
```python
import math

import jax
import jax.numpy as jnp
from jax import lax
from jax.sharding import PartitionSpec as P

QUERY_HEADS = 32
KEY_VALUE_HEADS = 4
HEAD_SIZE = 128


epsilon = 1e-06
rope_base = 1000000.0
masked_score = -1e30


def rms_rows(matrix, norm_gain):
    widened = matrix.astype(jnp.float32)
    inverse = lax.rsqrt(jnp.mean(widened * widened, axis=-1, keepdims=True) + epsilon)
    return (widened * inverse * norm_gain).astype(jnp.bfloat16)


def rotate(key_rows, positions, head_dim):
    row_count = key_rows.shape[0]
    split_heads = key_rows.reshape(row_count, -1, head_dim)
    half_dim = head_dim // 2
    inverse_freq = rope_base ** (-(jnp.arange(half_dim, dtype=jnp.float32) * (2.0 / head_dim)))
    angles = positions.astype(jnp.float32)[:, None] * inverse_freq[None, :]
    cosine = jnp.concatenate([jnp.cos(angles), jnp.cos(angles)], -1)[:, None, :]
    sine = jnp.concatenate([jnp.sin(angles), jnp.sin(angles)], -1)[:, None, :]
    turned = jnp.concatenate([-split_heads[..., half_dim:], split_heads[..., :half_dim]], -1)
    return (split_heads * cosine + turned * sine).reshape(row_count, -1)


def per_device(
    hidden,
    suffix_hidden,
    norm_gain,
    key_matrix,
    value_matrix,
    key_offset_bias,
    value_offset_bias,
    suffix_query_rows,
    slot_keys,
    slot_values,
    page_slot_table,
    split_page,
):
    ctx_index = lax.axis_index("ctx")
    queries = lax.all_gather(suffix_query_rows, "ctx", axis=0, tiled=True)
    front_rows = hidden.shape[0]
    suffix_rows = suffix_hidden.shape[0]
    page_size = slot_keys.shape[1]
    slot_count = slot_keys.shape[0]
    total_pages = page_slot_table.shape[0]
    prefix_len = total_pages * page_size
    normed = rms_rows(jnp.concatenate([hidden, suffix_hidden], 0), norm_gain)
    col_width = key_matrix.shape[1]

    def accumulate(block_rows):
        return jnp.dot(normed, block_rows, preferred_element_type=jnp.float32)

    key_acc = accumulate(lax.all_gather(key_matrix, "ctx", axis=0, tiled=True))
    value_acc = accumulate(lax.all_gather(value_matrix, "ctx", axis=0, tiled=True))
    front_pos = ctx_index * front_rows + jnp.arange(front_rows, dtype=jnp.int32)
    suffix_pos = prefix_len + ctx_index * suffix_rows + jnp.arange(suffix_rows, dtype=jnp.int32)
    new_keys = rotate(
        key_acc + key_offset_bias, jnp.concatenate([front_pos, suffix_pos], 0), HEAD_SIZE
    ).astype(jnp.bfloat16)
    new_values = (value_acc + value_offset_bias).astype(jnp.bfloat16)
    cut_pos = split_page[0] * page_size
    global_slot = ctx_index * slot_count + jnp.arange(slot_count, dtype=jnp.int32)
    page_index = jnp.arange(total_pages, dtype=jnp.int32)
    slot_hits = (page_slot_table[None, :] == global_slot[:, None]) & (
        page_index[None, :] >= split_page[0]
    )
    slot_live = jnp.max(slot_hits.astype(jnp.int32), axis=1) > 0
    every_key = jnp.concatenate(
        [new_keys[:front_rows], slot_keys.reshape(-1, col_width), new_keys[front_rows:]], 0
    )
    every_value = jnp.concatenate(
        [new_values[:front_rows], slot_values.reshape(-1, col_width), new_values[front_rows:]], 0
    )
    query_count = queries.shape[0]
    query_pos = prefix_len + jnp.arange(query_count, dtype=jnp.int32)
    prefix_seen = jnp.concatenate([front_pos < cut_pos, jnp.repeat(slot_live, page_size)], 0)
    suffix_seen = suffix_pos[None, :] <= query_pos[:, None]
    visible = jnp.concatenate(
        [jnp.broadcast_to(prefix_seen[None, :], (query_count, prefix_seen.shape[0])), suffix_seen],
        1,
    )
    visible_wide = visible[:, None, :]
    sharing_count = QUERY_HEADS // KEY_VALUE_HEADS
    local_heads = col_width // HEAD_SIZE
    grouped_heads = queries.reshape(query_count, local_heads, sharing_count, HEAD_SIZE)
    top_list = []
    total_list = []
    numer_list = []
    for current_head in range(local_heads):
        head_keys = every_key[:, current_head * HEAD_SIZE : (current_head + 1) * HEAD_SIZE]
        head_values = every_value[:, current_head * HEAD_SIZE : (current_head + 1) * HEAD_SIZE]
        scores = jnp.einsum(
            "qgd,ld->qgl",
            grouped_heads[:, current_head],
            head_keys,
            preferred_element_type=jnp.float32,
        ) * (1.0 / math.sqrt(HEAD_SIZE))
        scores = jnp.where(visible_wide, scores, masked_score)
        row_top = jnp.max(scores, axis=-1)
        expos = jnp.where(visible_wide, jnp.exp(scores - row_top[..., None]), 0.0)
        total_list.append(jnp.sum(expos, axis=-1))
        top_list.append(row_top)
        numer_list.append(
            jnp.einsum(
                "qgl,ld->qgd",
                expos.astype(jnp.bfloat16),
                head_values,
                preferred_element_type=jnp.float32,
            )
        )
    row_top = jnp.stack(top_list, 1)
    weight_total = jnp.stack(total_list, 1)
    numer = jnp.stack(numer_list, 1)
    global_top = lax.pmax(row_top, "ctx")
    factor = jnp.exp(row_top - global_top)
    own_total, own_numer = (
        lax.psum_scatter(
            (weight_total * factor).reshape(query_count, -1), "ctx", scatter_dimension=0, tiled=True
        ),
        lax.psum_scatter(
            (numer * factor[..., None]).reshape(query_count, -1),
            "ctx",
            scatter_dimension=0,
            tiled=True,
        ),
    )
    own_total = own_total.reshape(suffix_rows, local_heads, sharing_count)
    own_numer = own_numer.reshape(suffix_rows, local_heads, sharing_count, HEAD_SIZE)
    attended = (own_numer / own_total[..., None]).reshape(suffix_rows, -1).astype(jnp.bfloat16)
    return (new_keys[:front_rows], new_values[:front_rows], attended)


def solution(mesh):
    return jax.shard_map(
        per_device,
        mesh=mesh,
        in_specs=(
            P(("req", "ctx"), None),
            P(("req", "ctx"), None),
            P(),
            P("ctx", "tp"),
            P("ctx", "tp"),
            P("tp"),
            P("tp"),
            P(("req", "ctx"), "tp"),
            P(("req", "ctx"), None, "tp"),
            P(("req", "ctx"), None, "tp"),
            P("req"),
            P("req"),
        ),
        out_specs=(P(("req", "ctx"), "tp"), P(("req", "ctx"), "tp"), P(("req", "ctx"), "tp")),
        check_vma=False,
    )
```

profile of v0, /device:TPU:0, one launch (start us, length us, event | category | flops | bytes accessed | tf_op | source)
XLA Modules:
  0.0 279.1 jit_solution(18304694990570031270)
XLA Ops:
  7.3 0.7 all-gather.4.cloned.1.call-update
  8.0 0.7 all-gather.6.cloned.1.call-update
  8.8 0.3 multiply_cosine_fusion
  9.1 0.1 pad_maximum_fusion.3
  9.4 32.9 %all-gather = bf16[8,2,2048]{2,1,0:T(2,128)(2,1)S(1)} all-gather(bf16[1,2,2048]{2,1,0:T(2,128)(2,1)} %bitcast.87), channel_id=1, replica_groups=mesh['req'=2,'ctx'=8,'tp'=2] {'ctx'}, dimensions={0}, use_global_device_ids=true | all-gather | bytes 73728 | tf_op jit(solution)/shard_map/all_gather | solution.py:51
  43.0 0.8 convert_reduce_fusion
  44.0 1.2 dynamic-slice
  45.9 2.5 fusion
  48.5 38.2 %all-gather.4.cloned.1.call-done = bf16[8192,256]{1,0:T(8,128)(2,1)} async-done(((bf16[1024,256]{1,0:T(8,128)(2,1)}), bf16[8192,256]{1,0:T(8,128)(2,1)}) %all-gather.4.cloned.1.call-update) | async-done | bytes 4194320 | tf_op jit(solution)/shard_map/all_gather | solution.py:64
  86.7 3.1 %convolution_add_fusion.1 = f32[130,256]{1,0:T(8,128)S(1)} fusion(bf16[8192,256]{1,0:T(8,128)(2,1)} %all-gather.4.cloned.1.call-done, f32[256]{0:T(256)S(1)} %copy-done.7, f32[8192]{0:T(1024)S(1)} %copy-done.6, f32[130]{0:T(256)S(1)} %add_rsqrt_fusion, bf16[2,8192]{1,0:T(2,128)(2,1)S(1)} %copy-done.5, bf16[128,8192]{1,0:T(8,128)(2,1)S(1)} %copy-done), kind=kOutput, calls=%fused_computation.13 | convolution fusion | flops 552747520 | bytes 6491656 | tf_op jit(solution)/shard_map/dot_general | solution.py:62
  89.9 0.2 slice_negate_fusion
  90.1 0.2 maximum_multiply_fusion
  90.5 70.1 %all-gather.6.cloned.1.call-done = bf16[8192,256]{1,0:T(8,128)(2,1)} async-done(((bf16[1024,256]{1,0:T(8,128)(2,1)}), bf16[8192,256]{1,0:T(8,128)(2,1)}) %all-gather.6.cloned.1.call-update) | async-done | bytes 4194320 | tf_op jit(solution)/shard_map/all_gather | solution.py:65
  160.5 3.1 %fusion.7 = bf16[130,256]{1,0:T(8,128)(2,1)S(1)} fusion(bf16[8192,256]{1,0:T(8,128)(2,1)} %all-gather.6.cloned.1.call-done, f32[256]{0:T(256)S(1)} %copy-done.8, f32[8192]{0:T(1024)S(1)} %copy-done.6, f32[130]{0:T(256)S(1)} %add_rsqrt_fusion, bf16[2,8192]{1,0:T(2,128)(2,1)S(1)} %copy-done.5, bf16[128,8192]{1,0:T(8,128)(2,1)S(1)} %copy-done), kind=kOutput, calls=%fused_computation.14 | convolution fusion | flops 552780800 | bytes 6425096 | tf_op jit(solution)/shard_map/dot_general | solution.py:62
  163.7 0.3 fusion.27
  164.0 0.3 fusion.28
  164.3 0.3 convolution_bitcast_fusion
  164.6 0.3 fusion.8
  164.9 0.3 convolution_bitcast_fusion.1
  165.2 19.0 %pmax.7 = f32[16,2,8]{0,2,1:T(8,128)S(1)} all-reduce(f32[16,2,8]{0,2,1:T(8,128)S(1)} %pad_maximum_fusion.5), channel_id=1, replica_groups=mesh['req'=2,'ctx'=8,'tp'=2] {'ctx'}, use_global_device_ids=true, to_apply=%region_4.5 | all-reduce | flops 256 | bytes 2048 | tf_op jit(solution)/shard_map/pmax | solution.py:125
  184.3 17.8 %all-reduce.1 = f32[16,16]{1,0:T(8,128)S(1)} all-reduce(f32[16,16]{1,0:T(8,128)S(1)} %copy.33), channel_id=3, replica_groups=mesh['req'=2,'ctx'=8,'tp'=2] {'ctx'}, use_global_device_ids=true, to_apply=%region_8.9.clone | all-reduce | flops 256 | bytes 2048
  202.3 0.7 copy.52
  203.1 68.0 %all-reduce.4.cloned.1.call-done = f32[16,2048]{1,0:T(8,128)} async-done(((f32[16,2048]{1,0:T(8,128)}), f32[16,2048]{1,0:T(8,128)}) %all-reduce.4.cloned.1.call-update) | async-done | bytes 131088
  271.1 1.5 fusion.20
  (60 shorter events, 1.2 us)
Async XLA Ops:
  7.2 79.6 %copy-start.5 = (bf16[2,8192]{1,0:T(2,128)(2,1)S(1)}, bf16[2,8192]{1,0:T(2,128)(2,1)}, u32[]{:S(2)}) copy-start(bf16[2,8192]{1,0:T(2,128)(2,1)} %param.13) | copy-start | bytes 98308
  7.2 79.5 %copy-start = (bf16[128,8192]{1,0:T(8,128)(2,1)S(1)}, bf16[128,8192]{1,0:T(8,128)(2,1)}, u32[]{:S(2)}) copy-start(bf16[128,8192]{1,0:T(8,128)(2,1)} %param.12) | copy-start | bytes 6291460
  7.2 79.5 %copy-start.7 = (f32[256]{0:T(256)S(1)}, f32[256]{0:T(256)}, u32[]{:S(2)}) copy-start(f32[256]{0:T(256)} %param.17) | copy-start | bytes 3076
  7.2 79.5 %copy-start.6 = (f32[8192]{0:T(1024)S(1)}, f32[8192]{0:T(1024)}, u32[]{:S(2)}) copy-start(f32[8192]{0:T(1024)} %param.14) | copy-start | bytes 98308
  7.2 79.5 %all-gather.4.cloned.1.call-start = ((), (), s32[]{:S(2)}) async-start(), calls=%async_computation | async-start | bytes 4718592 | tf_op jit(solution)/shard_map/all_gather | solution.py:64
  7.9 152.6 %all-gather.6.cloned.1.call-start = ((), (), s32[]{:S(2)}) async-start(), calls=%async_computation.1 | async-start | bytes 4718592 | tf_op jit(solution)/shard_map/all_gather | solution.py:65
  8.7 262.4 %all-reduce.4.cloned.1.call-start = ((), (), s32[]{:S(2)}) async-start(), calls=%async_computation.2 | async-start | bytes 262144
  48.5 112.1 %copy-start.8 = (f32[256]{0:T(256)S(1)}, f32[256]{0:T(256)}, u32[]{:S(2)}) copy-start(f32[256]{0:T(256)} %param.18) | copy-start | bytes 3076
  90.4 73.2 %copy-start.3 = (bf16[128,256]{1,0:T(8,128)(2,1)}, bf16[128,256]{1,0:T(8,128)(2,1)S(1)}, u32[]{:S(2)}) copy-start(bf16[128,256]{1,0:T(8,128)(2,1)S(1)} %slice.52) | copy-start | bytes 196612
  90.4 73.2 %copy-start.1 = (bf16[4,128,256]{2,1,0:T(8,128)(2,1)S(1)}, bf16[4,128,256]{2,1,0:T(8,128)(2,1)}, u32[]{:S(2)}) copy-start(bf16[4,128,256]{2,1,0:T(8,128)(2,1)} %param.20) | copy-start | bytes 786436
  90.5 73.8 %copy-start.2 = (bf16[4,128,256]{2,1,0:T(8,128)(2,1)S(1)}, bf16[4,128,256]{2,1,0:T(8,128)(2,1)}, u32[]{:S(2)}) copy-start(bf16[4,128,256]{2,1,0:T(8,128)(2,1)} %param.21) | copy-start | bytes 786436
  163.6 109.0 %copy-start.4 = (bf16[128,256]{1,0:T(8,128)(2,1)}, bf16[128,256]{1,0:T(8,128)(2,1)S(1)}, u32[]{:S(2)}) copy-start(bf16[128,256]{1,0:T(8,128)(2,1)S(1)} %slice.53) | copy-start | bytes 196612
Sparse Core Ops, SparseCore 0:
  10.2 76.4 all-gather.3
  88.8 71.6 all-gather.5
  203.2 67.8 all-reduce.3
where the time goes:
time: 279 us
  waiting for transfers between devices  178 us (64%)
  blocking collectives  69.7 us (25%)
  between operations  15.5 us (6%)
  matrix products  7.25 us (3%)
  other arithmetic  6.25 us (2%)
    all_gather x1, waiting for transfers between devices, per_device(): lax.all_gather(value_matrix, 'ctx', axis=0, tiled=True)  70.1 us
    unnamed x4, waiting for transfers between devices  69.4 us
    all_gather x1, waiting for transfers between devices, per_device(): key_acc = accumulate(lax.all_gather(key_matrix, 'ctx', axis=0, tiled=True))  38.2 us
    all_gather x1, blocking collectives, per_device(): queries = lax.all_gather(suffix_query_rows, 'ctx', axis=0, tiled=True)  32.9 us
    pmax x1, blocking collectives, per_device(): global_top = lax.pmax(row_top, 'ctx')  19 us
    unnamed x1, blocking collectives  17.8 us
    dot_general x2, matrix products, accumulate(): return jnp.dot(normed, block_rows, preferred_element_type=jnp.float32)  6.12 us
  transfers between devices with their start and end apart: 3, of which 3 were waited for; matrix products, arithmetic and copies ran while one was open for 3% of the time, Pallas kernels for 0%

commit v1 on v0

--- a/solution.py
+++ b/solution.py
@@ -3,6 +3,8 @@
 import jax
 import jax.numpy as jnp
 from jax import lax
+from jax.experimental import pallas as pl
+from jax.experimental.pallas import tpu as pltpu
 from jax.sharding import PartitionSpec as P
 
 QUERY_HEADS = 32
@@ -33,7 +35,7 @@
     return (split_heads * cosine + turned * sine).reshape(row_count, -1)
 
 
-def per_device(
+def gathered_plan(
     hidden,
     suffix_hidden,
     norm_gain,
@@ -140,8 +142,412 @@
     attended = (own_numer / own_total[..., None]).reshape(suffix_rows, -1).astype(jnp.bfloat16)
     return (new_keys[:front_rows], new_values[:front_rows], attended)
 
+GROUPS = 4
+PAIR = 2
+LANES = 128
+SCALE = 1.0 / math.sqrt(HEAD_SIZE)
+
+
+def row_scale(values):
+    mean = jnp.sum(values * values, axis=-1, keepdims=True) * (1.0 / values.shape[-1])
+    return lax.rsqrt(mean + epsilon)
+
+
+def norm_kernel(place_ref, hidden_ref, suffix_ref, gain_ref, *rest):
+    outs, tail_ref = rest[:GROUPS], rest[GROUPS]
+    core, ctx = place_ref[0], place_ref[1]
+    z, x = ctx // PAIR, ctx % PAIR
+    step = pl.program_id(0)
+    rows = hidden_ref.shape[0]
+    half_rows = rows * pl.num_programs(0)
+    block = hidden_ref.shape[1] // (GROUPS * PAIR)
+    per_block = block // LANES
+    inverse = row_scale(hidden_ref[...].astype(jnp.float32))
+
+    def offset(shift, side, j):
+        owner = lax.rem(z + shift, GROUPS) * PAIR + lax.rem(x + side, PAIR)
+        return pl.multiple_of(owner * block + j * LANES, LANES)
+
+    for shift in range(GROUPS):
+        for side in range(PAIR):
+            for j in range(per_block):
+                columns = pl.ds(offset(shift, side, j), LANES)
+                piece = hidden_ref[:, columns].astype(jnp.float32) * inverse * gain_ref[:, columns]
+                start = pl.multiple_of((side * per_block + j) * half_rows + step * rows, rows)
+                outs[shift][pl.ds(start, rows), :] = piece.astype(jnp.bfloat16)
+
+    @pl.when(step == 0)
+    def _():
+        both = suffix_ref[...].astype(jnp.float32)
+        normed = both * row_scale(both) * gain_ref[...]
+        tail_ref[...] = jnp.where(core == 0, normed[0:1], normed[1:2])
+        for shift in range(GROUPS):
+            pieces = [
+                tail_ref[:, pl.ds(offset(shift, side, j), LANES)]
+                for side in range(PAIR)
+                for j in range(per_block)
+            ]
+            start = PAIR * per_block * half_rows
+            outs[shift][start : start + PAIR * per_block, :] = jnp.concatenate(pieces, 0).astype(
+                jnp.bfloat16
+            )
+
+
+def project_kernel(*refs):
+    blocks = refs[: 2 * GROUPS]
+    near_key, near_value, far_key, far_value = refs[2 * GROUPS : 2 * GROUPS + 4]
+    outs = refs[2 * GROUPS + 4 : 3 * GROUPS + 4]
+    lhs_ref = refs[3 * GROUPS + 4]
+    depth = near_key.shape[0]
+    pieces = 2 * depth // LANES
+    half_rows = (blocks[0].shape[0] - pieces) // pieces
+    rows = 2 * half_rows
+    tails = []
+    for i, block in enumerate(blocks):
+        for j in range(pieces):
+            lhs_ref[i * half_rows : (i + 1) * half_rows, j * LANES : (j + 1) * LANES] = block[
+                j * half_rows : (j + 1) * half_rows, :
+            ]
+        tail = block[pieces * half_rows :, :].astype(jnp.float32)
+        tails.append(jnp.concatenate([tail[j : j + 1] for j in range(pieces)], 1))
+    tails.append(jnp.zeros((16 - len(tails), 2 * depth), jnp.float32))
+    total = GROUPS * rows
+    lhs_ref[total : total + 16, :] = jnp.concatenate(tails, 0).astype(jnp.bfloat16)
+
+    def product(near, far):
+        return jnp.dot(
+            lhs_ref[:, :depth], near[...], preferred_element_type=jnp.float32
+        ) + jnp.dot(lhs_ref[:, depth:], far[...], preferred_element_type=jnp.float32)
+
+    keys = product(near_key, far_key)
+    values = product(near_value, far_value)
+    high = keys.astype(jnp.bfloat16).astype(jnp.float32)
+    low = keys - high
+    columns = []
+    for array in (high, low, values):
+        for j in range(array.shape[1] // LANES):
+            columns.append(array[:, j * LANES : (j + 1) * LANES])
+    for group in range(GROUPS):
+        for t, column in enumerate(columns):
+            outs[group][t * rows : (t + 1) * rows, :] = column[
+                group * rows : (group + 1) * rows
+            ].astype(jnp.bfloat16)
+        ends = [c[total + 2 * group : total + 2 * group + 2] for c in columns]
+        ends.append(jnp.zeros((16 - 2 * len(columns), LANES), jnp.float32))
+        outs[group][len(columns) * rows :, :] = jnp.concatenate(ends, 0).astype(jnp.bfloat16)
+
+
+def head_queries(query_ref, head, sharing):
+    start = head * sharing * HEAD_SIZE
+    return jnp.concatenate(
+        [query_ref[:, start + g * HEAD_SIZE : start + (g + 1) * HEAD_SIZE] for g in range(sharing)], 0
+    )
+
+
+def times_transposed(a, b):
+    return lax.dot_general(a, b, (((1,), (1,)), ((), ())), preferred_element_type=jnp.float32)
+
+
+def loaded_kernel(place_ref, table_ref, split_ref, query_ref, key_ref, value_ref, top_ref, total_ref, numer_ref):
+    ctx = place_ref[1]
+    slots, page, width = key_ref.shape
+    heads = width // HEAD_SIZE
+    sharing = query_ref.shape[1] // width
+    split = split_ref[0]
+    live = []
+    for s in range(slots):
+        hit = jnp.int32(0)
+        for p in range(table_ref.shape[0]):
+            hit = hit | ((table_ref[p] == ctx * slots + s) & (p >= split)).astype(jnp.int32)
+        live.append(hit)
+    for head in range(heads):
+        columns = slice(head * HEAD_SIZE, (head + 1) * HEAD_SIZE)
+        queries = head_queries(query_ref, head, sharing)
+        count = queries.shape[0]
+        scores = [
+            jnp.where(live[s] > 0, times_transposed(queries, key_ref[s, :, columns]) * SCALE, masked_score)
+            for s in range(slots)
+        ]
+        top = scores[0].max(-1, keepdims=True)
+        for s in range(1, slots):
+            top = jnp.maximum(top, scores[s].max(-1, keepdims=True))
+        total = jnp.zeros((count, 1), jnp.float32)
+        numer = jnp.zeros((count, HEAD_SIZE), jnp.float32)
+        for s in range(slots):
+            expos = jnp.where(live[s] > 0, jnp.exp(scores[s] - top), 0.0)
+            total += expos.sum(-1, keepdims=True)
+            numer += jnp.dot(
+                expos.astype(jnp.bfloat16), value_ref[s, :, columns], preferred_element_type=jnp.float32
+            )
+        rows = slice(head * count, (head + 1) * count)
+        top_ref[rows, :] = jnp.broadcast_to(top, (count, LANES))
+        total_ref[rows, :] = jnp.broadcast_to(total, (count, LANES))
+        numer_ref[rows, :] = numer
+
+
+def front_kernel(
+    place_ref, split_ref, own, *refs
+):
+    received = refs[: GROUPS - 1]
+    (key_bias, value_bias, cosine_ref, sine_ref, query_ref, top_ref, total_ref, numer_ref) = refs[
+        GROUPS - 1 : GROUPS + 7
+    ]
+    front_key, front_value = refs[GROUPS + 7 : GROUPS + 9]
+    outs = refs[GROUPS + 9 : -2]
+    state_ref, stat_ref = refs[-2:]
+    core, ctx = place_ref[0], place_ref[1]
+    rows, width = front_key.shape
+    half_rows = rows // 2
+    heads = width // HEAD_SIZE
+    n_ctx = len(outs)
+    query_count = query_ref.shape[0]
+    own_queries = query_count // n_ctx
+    sharing = query_ref.shape[1] // width
+    count = sharing * query_count
+    visible = ctx < split_ref[0]
+
+    def summed(start, size):
+        value = own[start : start + size, :].astype(jnp.float32)
+        for ref in received:
+            value += ref[start : start + size, :].astype(jnp.float32)
+        return value
+
+    ends = summed(3 * heads * rows, 16)
+    row_slot = lax.broadcasted_iota(jnp.int32, (count, 16), 0) % query_count
+    query_position = lax.rem(ctx - row_slot // own_queries + n_ctx, n_ctx) * own_queries + row_slot % own_queries
+    end_column = lax.broadcasted_iota(jnp.int32, (count, 16), 1)
+    end_position = ctx * 2 + jnp.where(end_column == 0, core, 1 - core)
+    end_seen = (end_column < 2) & (end_position <= query_position)
+    pad = jnp.zeros((14, HEAD_SIZE), jnp.float32)
+    for head in range(heads):
+        columns = slice(head * HEAD_SIZE, (head + 1) * HEAD_SIZE)
+        raw = summed(head * rows, rows) + summed((heads + head) * rows, rows)
+        value = (summed((2 * heads + head) * rows, rows) + value_bias[:, columns]).astype(jnp.bfloat16)
+        end_raw = ends[2 * head : 2 * head + 2] + ends[2 * (heads + head) : 2 * (heads + head) + 2]
+        end_value = ends[2 * (2 * heads + head) : 2 * (2 * heads + head) + 2] + value_bias[:, columns]
+        end_raw = jnp.concatenate([end_raw + key_bias[:, columns], pad], 0)
+        end_value = jnp.concatenate([end_value, pad], 0).astype(jnp.bfloat16)
+        raw = raw + key_bias[:, columns]
+
+        def rotated(k, part):
+            turned = pltpu.roll(k, HEAD_SIZE // 2, 1)
+            return (k * cosine_ref[part, :] + turned * sine_ref[part, :]).astype(jnp.bfloat16)
+
+        key = rotated(raw, slice(0, rows))
+        end_key = rotated(end_raw, slice(rows, rows + 16))
+        for half in range(2):
+            to = pl.ds(pl.multiple_of(lax.rem(core + half, 2) * half_rows, half_rows), half_rows)
+            front_key[to, columns] = key[half * half_rows : (half + 1) * half_rows]
+            front_value[to, columns] = value[half * half_rows : (half + 1) * half_rows]
+        queries = head_queries(query_ref, head, sharing)
+        scores = jnp.where(visible, times_transposed(queries, key) * SCALE, masked_score)
+        end_scores = jnp.where(end_seen, times_transposed(queries, end_key) * SCALE, masked_score)
+        part = slice(head * count, (head + 1) * count)
+        old_top = top_ref[part, :]
+        top = jnp.maximum(scores.max(-1, keepdims=True), end_scores.max(-1, keepdims=True))
+        top = jnp.maximum(old_top, top)
+        factor = jnp.exp(old_top - top)
+        expos = jnp.where(visible, jnp.exp(scores - top), 0.0)
+        end_expos = jnp.where(end_seen, jnp.exp(end_scores - top[:, :16]), 0.0)
+        total = total_ref[part, :] * factor + (
+            expos.sum(-1, keepdims=True) + end_expos.sum(-1, keepdims=True)
+        )
+        numer = (
+            numer_ref[part, :] * factor
+            + jnp.dot(expos.astype(jnp.bfloat16), value, preferred_element_type=jnp.float32)
+            + jnp.dot(end_expos.astype(jnp.bfloat16), end_value, preferred_element_type=jnp.float32)
+        )
+        state_ref[part, :] = numer
+        lane = lax.broadcasted_iota(jnp.int32, (count, LANES), 1)
+        stat_ref[part, :] = jnp.where(lane < LANES // 2, top, total)
+    query_heads = heads * sharing
+    for slot, out in enumerate(outs):
+        for i in range(own_queries):
+            pick = pl.ds(slot * own_queries + i, query_heads, stride=query_count)
+            out[i * query_heads : (i + 1) * query_heads, :] = state_ref[pick, :]
+            out[(own_queries + i) * query_heads : (own_queries + i + 1) * query_heads, :] = stat_ref[pick, :]
+
+
+def merge_kernel(*refs):
+    parts, out = refs[:-1], refs[-1]
+    rows = parts[0].shape[0] // 2
+    tops = [p[rows:, 0:1] for p in parts]
+    top = tops[0]
+    for t in tops[1:]:
+        top = jnp.maximum(top, t)
+    total = jnp.zeros((rows, 1), jnp.float32)
+    numer = jnp.zeros((rows, LANES), jnp.float32)
+    for p, t in zip(parts, tops):
+        factor = jnp.exp(t - top)
+        total += factor * p[rows:, LANES // 2 : LANES // 2 + 1]
+        numer += factor * p[:rows, :]
+    result = numer / total
+    queries = out.shape[0]
+    each = rows // queries
+    lines = [
+        jnp.concatenate([result[i * each + k : i * each + k + 1] for k in range(each)], 1)
+        for i in range(queries)
+    ]
+    out[...] = jnp.concatenate(lines, 0).astype(jnp.bfloat16)
+
+
+def exchange_plan(
+    hidden,
+    suffix_hidden,
+    norm_gain,
+    key_matrix,
+    value_matrix,
+    key_offset_bias,
+    value_offset_bias,
+    suffix_query_rows,
+    slot_keys,
+    slot_values,
+    page_slot_table,
+    split_page,
+):
+    n_ctx = GROUPS * PAIR
+    ctx = lax.axis_index("ctx").astype(jnp.int32)
+    core = lax.axis_index("tp").astype(jnp.int32)
+    place = jnp.stack([core, ctx])
+    rows, features = hidden.shape
+    half_rows = rows // 2
+    width = key_matrix.shape[1]
+    query_width = suffix_query_rows.shape[1]
+    prefix_len = page_slot_table.shape[0] * slot_keys.shape[1]
+    smem = pl.BlockSpec(memory_space=pltpu.SMEM)
+    vmem = pl.BlockSpec(memory_space=pltpu.VMEM)
+    params = pltpu.CompilerParams(vmem_limit_bytes=48 * 1024 * 1024)
+
+    def move(array, target):
+        pairs = []
+        for c in range(n_ctx):
+            for t in range(2):
+                to_c, to_t = target(c, t)
+                pairs.append((c * 2 + t, to_c * 2 + to_t))
+        return lax.ppermute(array, ("ctx", "tp"), pairs)
+
+    def around(shift):
+        return lambda c, t: ((c + shift) % n_ctx, t)
+
+    def along(shift):
+        return lambda c, t: ((c // PAIR + shift) % GROUPS * PAIR + c % PAIR, t)
+
+    def beside(c, t):
+        return (c ^ 1, t)
+
+    def sibling(c, t):
+        return (c, 1 - t)
+
+    query_parts = [suffix_query_rows] + [move(suffix_query_rows, around(s)) for s in range(1, n_ctx)]
+    far_key = move(key_matrix, beside)
+    far_value = move(value_matrix, beside)
+
+    steps = 4
+    pieces = features // GROUPS // LANES
+    block_rows = pieces * half_rows + pieces
+    blocks = pl.pallas_call(
+        norm_kernel,
+        grid_spec=pltpu.PrefetchScalarGridSpec(
+            num_scalar_prefetch=1,
+            grid=(steps,),
+            in_specs=[
+                pl.BlockSpec((half_rows // steps, features), lambda i, place: (place[0] * steps + i, 0)),
+                pl.BlockSpec((2, features), lambda i, place: (0, 0)),
+                pl.BlockSpec((1, features), lambda i, place: (0, 0)),
+            ],
+            out_specs=[pl.BlockSpec((block_rows, LANES), lambda i, place: (0, 0))] * GROUPS,
+            scratch_shapes=[pltpu.VMEM((1, features), jnp.float32)],
+        ),
+        out_shape=[jax.ShapeDtypeStruct((block_rows, LANES), jnp.bfloat16)] * GROUPS,
+        compiler_params=params,
+        cost_estimate=pl.CostEstimate(flops=4 * half_rows * features, bytes_accessed=2 * 2 * half_rows * features, transcendentals=0),
+        name="norm_rows",
+    )(place, hidden, suffix_hidden, norm_gain.reshape(1, features))
+
+    mine = [blocks[0]] + [move(blocks[s], along(s)) for s in range(1, GROUPS)]
+    lhs = []
+    for block in mine:
+        lhs += [block, move(block, sibling)]
+
+    queries = jnp.concatenate(query_parts, 0)
+    query_count = queries.shape[0]
+    states = query_count * query_width // HEAD_SIZE
+    state = jax.ShapeDtypeStruct((states, LANES), jnp.float32)
+    top, total, numer = pl.pallas_call(
+        loaded_kernel,
+        in_specs=[smem, smem, smem, vmem, vmem, vmem],
+        out_specs=[vmem] * 3,
+        out_shape=[state] * 3,
+        compiler_params=params,
+        cost_estimate=pl.CostEstimate(flops=4 * states * slot_keys.shape[0] * slot_keys.shape[1] * HEAD_SIZE, bytes_accessed=4 * slot_keys.size, transcendentals=states * 512),
+        name="loaded_attention",
+    )(place, page_slot_table, split_page, queries, slot_keys, slot_values)
+
+    inverse_freq = rope_base ** (
+        -(jnp.arange(HEAD_SIZE // 2, dtype=jnp.float32) * (2.0 / HEAD_SIZE))
+    )
+    row = jnp.arange(rows + 16, dtype=jnp.int32)
+    front_position = ctx * rows + (row + core * half_rows) % rows
+    end_position = prefix_len + ctx * 2 + jnp.where(row == rows, core, 1 - core)
+    position = jnp.where(row < rows, front_position, end_position)
+    angles = position.astype(jnp.float32)[:, None] * inverse_freq[None, :]
+    cosine, sine = jnp.cos(angles), jnp.sin(angles)
+    cosine = jnp.concatenate([cosine, cosine], 1)
+    sine = jnp.concatenate([-sine, sine], 1)
+
+    part_rows = 3 * (width // LANES) * rows + 16
+    partials = pl.pallas_call(
+        project_kernel,
+        in_specs=[vmem] * (2 * GROUPS + 4),
+        out_specs=[vmem] * GROUPS,
+        out_shape=[jax.ShapeDtypeStruct((part_rows, LANES), jnp.bfloat16)] * GROUPS,
+        scratch_shapes=[pltpu.VMEM((GROUPS * rows + 16, PAIR * features // n_ctx), jnp.bfloat16)],
+        compiler_params=params,
+        cost_estimate=pl.CostEstimate(flops=2 * GROUPS * rows * 2 * width * features // GROUPS, bytes_accessed=6 * 1024 * 1024, transcendentals=0),
+        name="project",
+    )(*lhs, key_matrix, value_matrix, far_key, far_value)
+    received = [move(partials[s], along(-s)) for s in range(1, GROUPS)]
+
+    own_queries = suffix_query_rows.shape[0]
+    payload = jax.ShapeDtypeStruct((2 * own_queries * query_width // HEAD_SIZE, LANES), jnp.float32)
+    row_shape = jax.ShapeDtypeStruct((rows, width), jnp.bfloat16)
+    front_key, front_value, *payloads = pl.pallas_call(
+        front_kernel,
+        in_specs=[smem, smem] + [vmem] * (GROUPS + 8),
+        out_specs=[vmem] * (2 + n_ctx),
+        out_shape=[row_shape] * 2 + [payload] * n_ctx,
+        scratch_shapes=[pltpu.VMEM((states, LANES), jnp.float32)] * 2,
+        compiler_params=params,
+        cost_estimate=pl.CostEstimate(flops=4 * states * rows * HEAD_SIZE, bytes_accessed=2 * 1024 * 1024, transcendentals=states * rows),
+        name="front_attention",
+    )(
+        place,
+        split_page,
+        partials[0],
+        *received,
+        key_offset_bias.reshape(1, width),
+        value_offset_bias.reshape(1, width),
+        cosine,
+        sine,
+        queries,
+        top,
+        total,
+        numer,
+    )
+    parts = [payloads[0]] + [move(payloads[s], around(-s)) for s in range(1, n_ctx)]
+    attended = pl.pallas_call(
+        merge_kernel,
+        in_specs=[vmem] * n_ctx,
+        out_specs=vmem,
+        out_shape=jax.ShapeDtypeStruct((own_queries, query_width), jnp.bfloat16),
+        compiler_params=params,
+        name="merge",
+    )(*parts)
+    return (front_key, front_value, attended)
+
 
 def solution(mesh):
+    per_device = exchange_plan if mesh.shape["ctx"] == GROUPS * PAIR else gathered_plan
     return jax.shard_map(
         per_device,
         mesh=mesh,

time: 279 us -> 89.8 us (0.32)
  waiting for transfers between devices: 178 us -> 32.3 us
  blocking collectives: 69.7 us -> 0 us
  starting transfers between devices: 0.11 us -> 40 us
  between operations: 15.5 us -> 1.46 us
  Pallas kernels: 0 us -> 9.11 us
  matrix products: 7.25 us -> 0 us
  other arithmetic: 6.25 us -> 0.54 us
  local copies, waits for them, and re-layouts: 2.67 us -> 6.07 us
    all_gather x2 -> x0, waiting for transfers between devices: 108 us -> none  [the longest x1 70.1 us: per_device(): lax.all_gather(value_matrix, 'ctx', axis=0, tiled=True)]
    unnamed x4 -> x0, waiting for transfers between devices: 69.4 us -> none
    ppermute x0 -> x26, starting transfers between devices: none -> 40 us  [move(): return lax.ppermute(array, ('ctx', 'tp'), pairs)]
    all_gather x1 -> x0, blocking collectives: 32.9 us -> none  [per_device(): queries = lax.all_gather(suffix_query_rows, 'ctx', axis=0, tiled=True)]
    ppermute x0 -> x26, waiting for transfers between devices: none -> 32.3 us  [move(): return lax.ppermute(array, ('ctx', 'tp'), pairs)]
    pmax x1 -> x0, blocking collectives: 19 us -> none  [per_device(): global_top = lax.pmax(row_top, 'ctx')]
    unnamed x1 -> x0, blocking collectives: 17.8 us -> none
    pallas_call x0 -> x5, Pallas kernels: none -> 9.11 us  [the longest x1 3.27 us: exchange_plan(): pl.pallas_call(project_kernel, in_specs=[vmem] * (2 * GROUPS + 4), out_sp...]
  transfers between devices with their start and end apart: 3 -> 26, of which waited for: 3 -> 9; matrix products, arithmetic and copies ran while one was open for 3% -> 1% of each run, Pallas kernels for 0% -> 5%
where the time goes in v1:
time: 89.8 us; the launch traced here: 89.4 us
  starting transfers between devices  40 us (45%)
  waiting for transfers between devices  32.3 us (36%)
  Pallas kernels  9.11 us (10%)
  local copies, waits for them, and re-layouts  6.07 us (7%)
  between operations  1.46 us (2%)
    ppermute x26, starting transfers between devices, move(): return lax.ppermute(array, ('ctx', 'tp'), pairs)  40 us
    ppermute x26, waiting for transfers between devices, move(): return lax.ppermute(array, ('ctx', 'tp'), pairs)  32.3 us
    unnamed x26, local copies, waits for them, and re-layouts  5.96 us
    pallas_call x1, Pallas kernels, exchange_plan(): pl.pallas_call(project_kernel, in_specs=[vmem] * (2 * GROUPS + 4), out_sp...  3.27 us
    pallas_call x1, Pallas kernels, exchange_plan(): pl.pallas_call(norm_kernel, grid_spec=pltpu.PrefetchScalarGridSpec(num_sc...  1.94 us
  transfers between devices with their start and end apart: 26, of which 9 were waited for; matrix products, arithmetic and copies ran while one was open for 1% of the time, Pallas kernels for 5%

profile of v1, /device:TPU:0, one launch (start us, length us, event | category | flops | bytes accessed | tf_op | source)
XLA Modules:
  0.0 89.4 jit_solution(9982832903289075208)
XLA Ops:
  0.7 1.6 %copy-done = bf16[128,8192]{1,0:T(8,128)(2,1)S(1)} copy-done((bf16[128,8192]{1,0:T(8,128)(2,1)S(1)}, bf16[128,8192]{1,0:T(8,128)(2,1)}, u32[]{:S(2)}) %copy-start) | copy-done | bytes 2097176
  3.8 1.9 %norm_rows.1 = (bf16[1040,128]{1,0:T(8,128)(2,1)S(1)}, bf16[1040,128]{1,0:T(8,128)(2,1)S(1)}, bf16[1040,128]{1,0:T(8,128)(2,1)S(1)}, bf16[1040,128]{1,0:T(8,128)(2,1)S(1)}) custom-call(s32[2]{0:T(128)S(1)} %pad_add_fusion.place_ref, bf16[128,8192]{1,0:T(8,128)(2,1)S(1)} %copy-done, bf16[2,8192]{1,0:T(2,128)(2,1)S(1)} %copy-done.7, f32[1,8192]{1,0:T(1,128)S(1)} %bitcast.5), custom_call_target="tpu_custom_call" | custom-call | flops 2097152 | bytes 2097152 | tf_op jit(solution)/shard_map/norm_rows/pallas_call | solution.py:448
  5.8 3.1 %collective-permute-start.1 = (bf16[1040,128]{1,0:T(8,128)(2,1)S(1)}, bf16[1040,128]{1,0:T(8,128)(2,1)S(1)}, u32[]{:S(2)}, u32[]{:S(2)}) collective-permute-start(bf16[1040,128]{1,0:T(8,128)(2,1)S(1)} %get-tuple-element.25), channel_id=1, source_target_pairs={{0,4},{1,5},{2,6},{3,7},{4,8},{5,9},{6,10},{7,11},{8,12},{9,13},{1... | collective-permute-start | bytes 798728 | tf_op jit(solution)/shard_map/ppermute | solution.py:427
  8.9 2.6 %collective-permute-start.3 = (bf16[1040,128]{1,0:T(8,128)(2,1)S(1)}, bf16[1040,128]{1,0:T(8,128)(2,1)S(1)}, u32[]{:S(2)}, u32[]{:S(2)}) collective-permute-start(bf16[1040,128]{1,0:T(8,128)(2,1)S(1)} %get-tuple-element.26), channel_id=1, source_target_pairs={{0,8},{1,9},{2,10},{3,11},{4,12},{5,13},{6,14},{7,15},{8,0},{9,1},... | collective-permute-start | bytes 798728 | tf_op jit(solution)/shard_map/ppermute | solution.py:427
  12.8 1.5 %collective-permute-start.7 = (bf16[1024,256]{1,0:T(8,128)(2,1)S(1)}, bf16[1024,256]{1,0:T(8,128)(2,1)S(1)}, u32[]{:S(2)}, u32[]{:S(2)}) collective-permute-start(bf16[1024,256]{1,0:T(8,128)(2,1)S(1)} %copy-done.1), channel_id=1, source_target_pairs={{0,2},{1,3},{2,0},{3,1},{4,6},{5,7},{6,4},{7,5},{8,10},{9,11},{10,... | collective-permute-start | bytes 1572872 | tf_op jit(solution)/shard_map/ppermute | solution.py:427
  14.3 4.0 %collective-permute-done.1.refs_2_ = bf16[1040,128]{1,0:T(8,128)(2,1)S(1)} collective-permute-done((bf16[1040,128]{1,0:T(8,128)(2,1)S(1)}, bf16[1040,128]{1,0:T(8,128)(2,1)S(1)}, u32[]{:S(2)}, u32[]{:S(2)}) %collective-permute-start.1) | collective-permute-done | bytes 266272 | tf_op jit(solution)/shard_map/ppermute | solution.py:427
  18.3 1.7 %collective-permute-start.8 = (bf16[1024,256]{1,0:T(8,128)(2,1)S(1)}, bf16[1024,256]{1,0:T(8,128)(2,1)S(1)}, u32[]{:S(2)}, u32[]{:S(2)}) collective-permute-start(bf16[1024,256]{1,0:T(8,128)(2,1)S(1)} %copy-done.2), channel_id=1, source_target_pairs={{0,2},{1,3},{2,0},{3,1},{4,6},{5,7},{6,4},{7,5},{8,10},{9,11},{10,... | collective-permute-start | bytes 1572872 | tf_op jit(solution)/shard_map/ppermute | solution.py:427
  20.0 8.8 %collective-permute-done.3.refs_4_ = bf16[1040,128]{1,0:T(8,128)(2,1)S(1)} collective-permute-done((bf16[1040,128]{1,0:T(8,128)(2,1)S(1)}, bf16[1040,128]{1,0:T(8,128)(2,1)S(1)}, u32[]{:S(2)}, u32[]{:S(2)}) %collective-permute-start.3) | collective-permute-done | bytes 266272 | tf_op jit(solution)/shard_map/ppermute | solution.py:427
  29.5 1.5 %collective-permute-start.12 = (bf16[2,2048]{1,0:T(2,128)(2,1)S(1)}, bf16[2,2048]{1,0:T(2,128)(2,1)S(1)}, u32[]{:S(2)}, u32[]{:S(2)}) collective-permute-start(bf16[2,2048]{1,0:T(2,128)(2,1)S(1)} %copy-done.12), channel_id=1, source_target_pairs={{0,2},{1,3},{2,4},{3,5},{4,6},{5,7},{6,8},{7,9},{8,10},{9,11},{10,... | collective-permute-start | bytes 24584 | tf_op jit(solution)/shard_map/ppermute | solution.py:427
  31.0 7.3 %collective-permute-done.8.refs_11_ = bf16[1024,256]{1,0:T(8,128)(2,1)S(1)} collective-permute-done((bf16[1024,256]{1,0:T(8,128)(2,1)S(1)}, bf16[1024,256]{1,0:T(8,128)(2,1)S(1)}, u32[]{:S(2)}, u32[]{:S(2)}) %collective-permute-start.8) | collective-permute-done | bytes 524320 | tf_op jit(solution)/shard_map/ppermute | solution.py:427
  39.1 2.3 %collective-permute-start.14 = (bf16[2,2048]{1,0:T(2,128)(2,1)S(1)}, bf16[2,2048]{1,0:T(2,128)(2,1)S(1)}, u32[]{:S(2)}, u32[]{:S(2)}) collective-permute-start(bf16[2,2048]{1,0:T(2,128)(2,1)S(1)} %copy-done.12), channel_id=1, source_target_pairs={{0,6},{1,7},{2,8},{3,9},{4,10},{5,11},{6,12},{7,13},{8,14},{9,15},... | collective-permute-start | bytes 24584 | tf_op jit(solution)/shard_map/ppermute | solution.py:427
  41.3 2.5 %collective-permute-start.15 = (bf16[2,2048]{1,0:T(2,128)(2,1)S(1)}, bf16[2,2048]{1,0:T(2,128)(2,1)S(1)}, u32[]{:S(2)}, u32[]{:S(2)}) collective-permute-start(bf16[2,2048]{1,0:T(2,128)(2,1)S(1)} %copy-done.12), channel_id=1, source_target_pairs={{0,8},{1,9},{2,10},{3,11},{4,12},{5,13},{6,14},{7,15},{8,0},{9,1},... | collective-permute-start | bytes 24584 | tf_op jit(solution)/shard_map/ppermute | solution.py:427
  43.8 3.3 %project.1 = (bf16[784,128]{1,0:T(8,128)(2,1)S(1)}, bf16[784,128]{1,0:T(8,128)(2,1)}, bf16[784,128]{1,0:T(8,128)(2,1)}, bf16[784,128]{1,0:T(8,128)(2,1)}) custom-call(bf16[1040,128]{1,0:T(8,128)(2,1)S(1)} %get-tuple-element.24.refs_0_, bf16[1040,128]{1,0:T(8,128)(2,1)S(1)} %collective-permute-done.refs_1_, ...), custom_call_target="tpu_custom_call" | custom-call | flops 1073741824 | bytes 6291456 | tf_op jit(solution)/shard_map/project/pallas_call | solution.py:499
  47.1 2.0 %collective-permute-start.10 = (bf16[784,128]{1,0:T(8,128)(2,1)}, bf16[784,128]{1,0:T(8,128)(2,1)S(1)}, u32[]{:S(2)}, u32[]{:S(2)}) collective-permute-start(bf16[784,128]{1,0:T(8,128)(2,1)} %get-tuple-element.30), channel_id=1, source_target_pairs={{0,8},{1,9},{2,10},{3,11},{4,12},{5,13},{6,14},{7,15},{8,0},{9,1},... | collective-permute-start | bytes 602120 | tf_op jit(solution)/shard_map/ppermute | solution.py:427
  50.5 2.4 %collective-permute-start.9 = (bf16[784,128]{1,0:T(8,128)(2,1)}, bf16[784,128]{1,0:T(8,128)(2,1)S(1)}, u32[]{:S(2)}, u32[]{:S(2)}) collective-permute-start(bf16[784,128]{1,0:T(8,128)(2,1)} %get-tuple-element.29), channel_id=1, source_target_pairs={{0,12},{1,13},{2,14},{3,15},{4,0},{5,1},{6,2},{7,3},{8,4},{9,5},{1... | collective-permute-start | bytes 602120 | tf_op jit(solution)/shard_map/ppermute | solution.py:427
  55.7 5.2 %collective-permute-done.17 = bf16[2,2048]{1,0:T(2,128)(2,1)S(1)} collective-permute-done((bf16[2,2048]{1,0:T(2,128)(2,1)S(1)}, bf16[2,2048]{1,0:T(2,128)(2,1)S(1)}, u32[]{:S(2)}, u32[]{:S(2)}) %collective-permute-start.17) | collective-permute-done | bytes 8224 | tf_op jit(solution)/shard_map/ppermute | solution.py:427
  65.6 1.7 %front_attention.1 = (bf16[128,256]{1,0:T(8,128)(2,1)}, bf16[128,256]{1,0:T(8,128)(2,1)}, f32[64,128]{1,0:T(8,128)S(1)}, f32[64,128]{1,0:T(8,128)S(1)}, f32[64,1...) custom-call(s32[2]{0:T(128)S(1)} %pad_add_fusion.place_ref, ...), custom_call_target="tpu_custom_call" | custom-call | flops 16777216 | bytes 2097152 | tf_op jit(solution)/shard_map/front_attention/pallas_call | solution.py:514
  67.3 5.1 %collective-permute-start.19 = (f32[64,128]{1,0:T(8,128)S(1)}, f32[64,128]{1,0:T(8,128)S(1)}, u32[]{:S(2)}, u32[]{:S(2)}) collective-permute-start(f32[64,128]{1,0:T(8,128)S(1)} %get-tuple-element.38), channel_id=1, source_target_pairs={{0,14},{1,15},{2,0},{3,1},{4,2},{5,3},{6,4},{7,5},{8,6},{9,7},{10,... | collective-permute-start | bytes 98312 | tf_op jit(solution)/shard_map/ppermute | solution.py:427
  72.4 2.4 %collective-permute-start.20 = (f32[64,128]{1,0:T(8,128)S(1)}, f32[64,128]{1,0:T(8,128)S(1)}, u32[]{:S(2)}, u32[]{:S(2)}) collective-permute-start(f32[64,128]{1,0:T(8,128)S(1)} %get-tuple-element.39), channel_id=1, source_target_pairs={{0,12},{1,13},{2,14},{3,15},{4,0},{5,1},{6,2},{7,3},{8,4},{9,5},{1... | collective-permute-start | bytes 98312 | tf_op jit(solution)/shard_map/ppermute | solution.py:427
  74.8 1.8 %collective-permute-start.21 = (f32[64,128]{1,0:T(8,128)S(1)}, f32[64,128]{1,0:T(8,128)S(1)}, u32[]{:S(2)}, u32[]{:S(2)}) collective-permute-start(f32[64,128]{1,0:T(8,128)S(1)} %get-tuple-element.40), channel_id=1, source_target_pairs={{0,10},{1,11},{2,12},{3,13},{4,14},{5,15},{6,0},{7,1},{8,2},{9,3},... | collective-permute-start | bytes 98312 | tf_op jit(solution)/shard_map/ppermute | solution.py:427
  76.7 2.4 %collective-permute-start.23 = (f32[64,128]{1,0:T(8,128)S(1)}, f32[64,128]{1,0:T(8,128)S(1)}, u32[]{:S(2)}, u32[]{:S(2)}) collective-permute-start(f32[64,128]{1,0:T(8,128)S(1)} %get-tuple-element.42), channel_id=1, source_target_pairs={{0,6},{1,7},{2,8},{3,9},{4,10},{5,11},{6,12},{7,13},{8,14},{9,15},... | collective-permute-start | bytes 98312 | tf_op jit(solution)/shard_map/ppermute | solution.py:427
  79.1 2.9 %collective-permute-start.24 = (f32[64,128]{1,0:T(8,128)S(1)}, f32[64,128]{1,0:T(8,128)S(1)}, u32[]{:S(2)}, u32[]{:S(2)}) collective-permute-start(f32[64,128]{1,0:T(8,128)S(1)} %get-tuple-element.43), channel_id=1, source_target_pairs={{0,4},{1,5},{2,6},{3,7},{4,8},{5,9},{6,10},{7,11},{8,12},{9,13},{1... | collective-permute-start | bytes 98312 | tf_op jit(solution)/shard_map/ppermute | solution.py:427
  82.0 2.4 %collective-permute-done.23.refs_5_ = f32[64,128]{1,0:T(8,128)S(1)} collective-permute-done((f32[64,128]{1,0:T(8,128)S(1)}, f32[64,128]{1,0:T(8,128)S(1)}, u32[]{:S(2)}, u32[]{:S(2)}) %collective-permute-start.23) | collective-permute-done | bytes 32800 | tf_op jit(solution)/shard_map/ppermute | solution.py:427
  84.8 3.8 %collective-permute-done.25.refs_7_ = f32[64,128]{1,0:T(8,128)S(1)} collective-permute-done((f32[64,128]{1,0:T(8,128)S(1)}, f32[64,128]{1,0:T(8,128)S(1)}, u32[]{:S(2)}, u32[]{:S(2)}) %collective-permute-start.25) | collective-permute-done | bytes 32800 | tf_op jit(solution)/shard_map/ppermute | solution.py:427
  (65 shorter events, 13.7 us)
Async XLA Ops:
  5.8 12.5 %collective-permute-start.1 = (bf16[1040,128]{1,0:T(8,128)(2,1)S(1)}, bf16[1040,128]{1,0:T(8,128)(2,1)S(1)}, u32[]{:S(2)}, u32[]{:S(2)}) collective-permute-start(bf16[1040,128]{1,0:T(8,128)(2,1)S(1)} %get-tuple-element.25), channel_id=1, source_target_pairs={{0,4},{1,5},{2,6},{3,7},{4,8},{5,9},{6,10},{7,11},{8,12},{9,13},{1... | collective-permute-start | bytes 798728 | tf_op jit(solution)/shard_map/ppermute | solution.py:427
  8.9 20.0 %collective-permute-start.3 = (bf16[1040,128]{1,0:T(8,128)(2,1)S(1)}, bf16[1040,128]{1,0:T(8,128)(2,1)S(1)}, u32[]{:S(2)}, u32[]{:S(2)}) collective-permute-start(bf16[1040,128]{1,0:T(8,128)(2,1)S(1)} %get-tuple-element.26), channel_id=1, source_target_pairs={{0,8},{1,9},{2,10},{3,11},{4,12},{5,13},{6,14},{7,15},{8,0},{9,1},... | collective-permute-start | bytes 798728 | tf_op jit(solution)/shard_map/ppermute | solution.py:427
  11.5 17.4 %collective-permute-start.5 = (bf16[1040,128]{1,0:T(8,128)(2,1)S(1)}, bf16[1040,128]{1,0:T(8,128)(2,1)S(1)}, u32[]{:S(2)}, u32[]{:S(2)}) collective-permute-start(bf16[1040,128]{1,0:T(8,128)(2,1)S(1)} %get-tuple-element.27), channel_id=1, source_target_pairs={{0,12},{1,13},{2,14},{3,15},{4,0},{5,1},{6,2},{7,3},{8,4},{9,5},{1... | collective-permute-start | bytes 798728 | tf_op jit(solution)/shard_map/ppermute | solution.py:427
  12.8 16.5 %collective-permute-start = (bf16[1040,128]{1,0:T(8,128)(2,1)S(1)}, bf16[1040,128]{1,0:T(8,128)(2,1)S(1)}, u32[]{:S(2)}, u32[]{:S(2)}) collective-permute-start(bf16[1040,128]{1,0:T(8,128)(2,1)S(1)} %get-tuple-element.24.refs_0_), channel_id=1, source_target_pairs={{0,1},{1,0},{2,3},{3,2},{4,5},{5,4},{6,7},{7,6},{8,9},{9,8},{10,11... | collective-permute-start | bytes 798728 | tf_op jit(solution)/shard_map/ppermute | solution.py:427
  12.8 16.7 %collective-permute-start.7 = (bf16[1024,256]{1,0:T(8,128)(2,1)S(1)}, bf16[1024,256]{1,0:T(8,128)(2,1)S(1)}, u32[]{:S(2)}, u32[]{:S(2)}) collective-permute-start(bf16[1024,256]{1,0:T(8,128)(2,1)S(1)} %copy-done.1), channel_id=1, source_target_pairs={{0,2},{1,3},{2,0},{3,1},{4,6},{5,7},{6,4},{7,5},{8,10},{9,11},{10,... | collective-permute-start | bytes 1572872 | tf_op jit(solution)/shard_map/ppermute | solution.py:427
  18.3 20.1 %collective-permute-start.8 = (bf16[1024,256]{1,0:T(8,128)(2,1)S(1)}, bf16[1024,256]{1,0:T(8,128)(2,1)S(1)}, u32[]{:S(2)}, u32[]{:S(2)}) collective-permute-start(bf16[1024,256]{1,0:T(8,128)(2,1)S(1)} %copy-done.2), channel_id=1, source_target_pairs={{0,2},{1,3},{2,0},{3,1},{4,6},{5,7},{6,4},{7,5},{8,10},{9,11},{10,... | collective-permute-start | bytes 1572872 | tf_op jit(solution)/shard_map/ppermute | solution.py:427
  28.8 10.2 %collective-permute-start.2 = (bf16[1040,128]{1,0:T(8,128)(2,1)S(1)}, bf16[1040,128]{1,0:T(8,128)(2,1)}, u32[]{:S(2)}, u32[]{:S(2)}) collective-permute-start(bf16[1040,128]{1,0:T(8,128)(2,1)S(1)} %collective-permute-done.1.refs_2_), channel_id=1, source_target_pairs={{0,1},{1,0},{2,3},{3,2},{4,5},{5,4},{6,7},{7,6},{8,9},{9,8},{10,11... | collective-permute-start | bytes 798728 | tf_op jit(solution)/shard_map/ppermute | solution.py:427
  28.8 12.5 %collective-permute-start.4 = (bf16[1040,128]{1,0:T(8,128)(2,1)S(1)}, bf16[1040,128]{1,0:T(8,128)(2,1)}, u32[]{:S(2)}, u32[]{:S(2)}) collective-permute-start(bf16[1040,128]{1,0:T(8,128)(2,1)S(1)} %collective-permute-done.3.refs_4_), channel_id=1, source_target_pairs={{0,1},{1,0},{2,3},{3,2},{4,5},{5,4},{6,7},{7,6},{8,9},{9,8},{10,11... | collective-permute-start | bytes 798728 | tf_op jit(solution)/shard_map/ppermute | solution.py:427
  29.3 14.4 %collective-permute-start.6 = (bf16[1040,128]{1,0:T(8,128)(2,1)S(1)}, bf16[1040,128]{1,0:T(8,128)(2,1)}, u32[]{:S(2)}, u32[]{:S(2)}) collective-permute-start(bf16[1040,128]{1,0:T(8,128)(2,1)S(1)} %collective-permute-done.5.refs_6_), channel_id=1, source_target_pairs={{0,1},{1,0},{2,3},{3,2},{4,5},{5,4},{6,7},{7,6},{8,9},{9,8},{10,11... | collective-permute-start | bytes 798728 | tf_op jit(solution)/shard_map/ppermute | solution.py:427
  29.5 17.6 %collective-permute-start.12 = (bf16[2,2048]{1,0:T(2,128)(2,1)S(1)}, bf16[2,2048]{1,0:T(2,128)(2,1)S(1)}, u32[]{:S(2)}, u32[]{:S(2)}) collective-permute-start(bf16[2,2048]{1,0:T(2,128)(2,1)S(1)} %copy-done.12), channel_id=1, source_target_pairs={{0,2},{1,3},{2,4},{3,5},{4,6},{5,7},{6,8},{7,9},{8,10},{9,11},{10,... | collective-permute-start | bytes 24584 | tf_op jit(solution)/shard_map/ppermute | solution.py:427
  38.4 10.7 %collective-permute-start.13 = (bf16[2,2048]{1,0:T(2,128)(2,1)S(1)}, bf16[2,2048]{1,0:T(2,128)(2,1)S(1)}, u32[]{:S(2)}, u32[]{:S(2)}) collective-permute-start(bf16[2,2048]{1,0:T(2,128)(2,1)S(1)} %copy-done.12), channel_id=1, source_target_pairs={{0,4},{1,5},{2,6},{3,7},{4,8},{5,9},{6,10},{7,11},{8,12},{9,13},{1... | collective-permute-start | bytes 24584 | tf_op jit(solution)/shard_map/ppermute | solution.py:427
  39.1 11.5 %collective-permute-start.14 = (bf16[2,2048]{1,0:T(2,128)(2,1)S(1)}, bf16[2,2048]{1,0:T(2,128)(2,1)S(1)}, u32[]{:S(2)}, u32[]{:S(2)}) collective-permute-start(bf16[2,2048]{1,0:T(2,128)(2,1)S(1)} %copy-done.12), channel_id=1, source_target_pairs={{0,6},{1,7},{2,8},{3,9},{4,10},{5,11},{6,12},{7,13},{8,14},{9,15},... | collective-permute-start | bytes 24584 | tf_op jit(solution)/shard_map/ppermute | solution.py:427
  41.3 11.9 %collective-permute-start.15 = (bf16[2,2048]{1,0:T(2,128)(2,1)S(1)}, bf16[2,2048]{1,0:T(2,128)(2,1)S(1)}, u32[]{:S(2)}, u32[]{:S(2)}) collective-permute-start(bf16[2,2048]{1,0:T(2,128)(2,1)S(1)} %copy-done.12), channel_id=1, source_target_pairs={{0,8},{1,9},{2,10},{3,11},{4,12},{5,13},{6,14},{7,15},{8,0},{9,1},... | collective-permute-start | bytes 24584 | tf_op jit(solution)/shard_map/ppermute | solution.py:427
  43.8 10.9 %collective-permute-start.16 = (bf16[2,2048]{1,0:T(2,128)(2,1)S(1)}, bf16[2,2048]{1,0:T(2,128)(2,1)S(1)}, u32[]{:S(2)}, u32[]{:S(2)}) collective-permute-start(bf16[2,2048]{1,0:T(2,128)(2,1)S(1)} %copy-done.12), channel_id=1, source_target_pairs={{0,10},{1,11},{2,12},{3,13},{4,14},{5,15},{6,0},{7,1},{8,2},{9,3},... | collective-permute-start | bytes 24584 | tf_op jit(solution)/shard_map/ppermute | solution.py:427
  47.1 17.5 %collective-permute-start.10 = (bf16[784,128]{1,0:T(8,128)(2,1)}, bf16[784,128]{1,0:T(8,128)(2,1)S(1)}, u32[]{:S(2)}, u32[]{:S(2)}) collective-permute-start(bf16[784,128]{1,0:T(8,128)(2,1)} %get-tuple-element.30), channel_id=1, source_target_pairs={{0,8},{1,9},{2,10},{3,11},{4,12},{5,13},{6,14},{7,15},{8,0},{9,1},... | collective-permute-start | bytes 602120 | tf_op jit(solution)/shard_map/ppermute | solution.py:427
  49.1 15.5 %collective-permute-start.11 = (bf16[784,128]{1,0:T(8,128)(2,1)}, bf16[784,128]{1,0:T(8,128)(2,1)S(1)}, u32[]{:S(2)}, u32[]{:S(2)}) collective-permute-start(bf16[784,128]{1,0:T(8,128)(2,1)} %get-tuple-element.31), channel_id=1, source_target_pairs={{0,4},{1,5},{2,6},{3,7},{4,8},{5,9},{6,10},{7,11},{8,12},{9,13},{1... | collective-permute-start | bytes 602120 | tf_op jit(solution)/shard_map/ppermute | solution.py:427
  50.5 14.1 %collective-permute-start.9 = (bf16[784,128]{1,0:T(8,128)(2,1)}, bf16[784,128]{1,0:T(8,128)(2,1)S(1)}, u32[]{:S(2)}, u32[]{:S(2)}) collective-permute-start(bf16[784,128]{1,0:T(8,128)(2,1)} %get-tuple-element.29), channel_id=1, source_target_pairs={{0,12},{1,13},{2,14},{3,15},{4,0},{5,1},{6,2},{7,3},{8,4},{9,5},{1... | collective-permute-start | bytes 602120 | tf_op jit(solution)/shard_map/ppermute | solution.py:427
  53.3 7.7 %collective-permute-start.17 = (bf16[2,2048]{1,0:T(2,128)(2,1)S(1)}, bf16[2,2048]{1,0:T(2,128)(2,1)S(1)}, u32[]{:S(2)}, u32[]{:S(2)}) collective-permute-start(bf16[2,2048]{1,0:T(2,128)(2,1)S(1)} %copy-done.12), channel_id=1, source_target_pairs={{0,12},{1,13},{2,14},{3,15},{4,0},{5,1},{6,2},{7,3},{8,4},{9,5},{1... | collective-permute-start | bytes 24584 | tf_op jit(solution)/shard_map/ppermute | solution.py:427
  54.7 6.3 %collective-permute-start.18 = (bf16[2,2048]{1,0:T(2,128)(2,1)S(1)}, bf16[2,2048]{1,0:T(2,128)(2,1)S(1)}, u32[]{:S(2)}, u32[]{:S(2)}) collective-permute-start(bf16[2,2048]{1,0:T(2,128)(2,1)S(1)} %copy-done.12), channel_id=1, source_target_pairs={{0,14},{1,15},{2,0},{3,1},{4,2},{5,3},{6,4},{7,5},{8,6},{9,7},{10,... | collective-permute-start | bytes 24584 | tf_op jit(solution)/shard_map/ppermute | solution.py:427
  67.3 11.8 %collective-permute-start.19 = (f32[64,128]{1,0:T(8,128)S(1)}, f32[64,128]{1,0:T(8,128)S(1)}, u32[]{:S(2)}, u32[]{:S(2)}) collective-permute-start(f32[64,128]{1,0:T(8,128)S(1)} %get-tuple-element.38), channel_id=1, source_target_pairs={{0,14},{1,15},{2,0},{3,1},{4,2},{5,3},{6,4},{7,5},{8,6},{9,7},{10,... | collective-permute-start | bytes 98312 | tf_op jit(solution)/shard_map/ppermute | solution.py:427
  72.4 9.6 %collective-permute-start.20 = (f32[64,128]{1,0:T(8,128)S(1)}, f32[64,128]{1,0:T(8,128)S(1)}, u32[]{:S(2)}, u32[]{:S(2)}) collective-permute-start(f32[64,128]{1,0:T(8,128)S(1)} %get-tuple-element.39), channel_id=1, source_target_pairs={{0,12},{1,13},{2,14},{3,15},{4,0},{5,1},{6,2},{7,3},{8,4},{9,5},{1... | collective-permute-start | bytes 98312 | tf_op jit(solution)/shard_map/ppermute | solution.py:427
  74.8 7.2 %collective-permute-start.21 = (f32[64,128]{1,0:T(8,128)S(1)}, f32[64,128]{1,0:T(8,128)S(1)}, u32[]{:S(2)}, u32[]{:S(2)}) collective-permute-start(f32[64,128]{1,0:T(8,128)S(1)} %get-tuple-element.40), channel_id=1, source_target_pairs={{0,10},{1,11},{2,12},{3,13},{4,14},{5,15},{6,0},{7,1},{8,2},{9,3},... | collective-permute-start | bytes 98312 | tf_op jit(solution)/shard_map/ppermute | solution.py:427
  76.7 7.7 %collective-permute-start.23 = (f32[64,128]{1,0:T(8,128)S(1)}, f32[64,128]{1,0:T(8,128)S(1)}, u32[]{:S(2)}, u32[]{:S(2)}) collective-permute-start(f32[64,128]{1,0:T(8,128)S(1)} %get-tuple-element.42), channel_id=1, source_target_pairs={{0,6},{1,7},{2,8},{3,9},{4,10},{5,11},{6,12},{7,13},{8,14},{9,15},... | collective-permute-start | bytes 98312 | tf_op jit(solution)/shard_map/ppermute | solution.py:427
  82.0 6.6 %collective-permute-start.25 = (f32[64,128]{1,0:T(8,128)S(1)}, f32[64,128]{1,0:T(8,128)S(1)}, u32[]{:S(2)}, u32[]{:S(2)}) collective-permute-start(f32[64,128]{1,0:T(8,128)S(1)} %get-tuple-element.44), channel_id=1, source_target_pairs={{0,2},{1,3},{2,4},{3,5},{4,6},{5,7},{6,8},{7,9},{8,10},{9,11},{10,... | collective-permute-start | bytes 98312 | tf_op jit(solution)/shard_map/ppermute | solution.py:427
  (15 other events, 185.2 us)
